TPU v7x, 32 devices: a whole 2x2x4 slice. The times are simulated.
32 devices in a mesh: site: 32 (over z, y, x, core).
Axes of the slice: x: 2, y: 2, z: 4, core: 2. Of those that a mesh axis runs over, the one named last changes fastest.
Arguments:
- site_tensors: bfloat16 [32, 256, 8, 256], P('site'), may hold values from -1.5 to 1.5
- first_gates: bfloat16 [32, 64, 64], P('site'), may hold values from -0.75 to 0.75
- second_gates: bfloat16 [32, 64, 64], P('site'), may hold values from -0.75 to 0.75
- first_sketch: int32 [32, 2048, 256], P('site'), may hold values from -1 to 1
- second_sketch: int32 [32, 2048, 256], P('site'), may hold values from -1 to 1
Outputs:
- evolved: bfloat16 [32, 256, 8, 256], P('site')
All inputs are finite; a program needn't handle non-finite values.
Results may differ from a plain program's by a relative error of at most 0.018.
Values may be sent and summed in bfloat16 or wider, within the bound.
A program may use at most 64 MiB of HBM per device.

v0:
```python
import jax
import jax.numpy as jnp
from jax import lax
from jax.sharding import PartitionSpec as P


def from_behind(array, axis, by):
    size = lax.axis_size(axis)
    pairs = [(i, i + by) for i in range(size) if 0 <= i + by < size]
    return lax.ppermute(array, axis, pairs)


def contract(row_block, partner, gate_matrix):
    bond_dim = partner.shape[0]
    levels = partner.shape[1]
    rows_count = row_block.shape[0]
    two_site = jnp.dot(
        row_block.reshape(rows_count * levels, bond_dim),
        partner.reshape(bond_dim, levels * bond_dim),
        preferred_element_type=jnp.float32,
    ).astype(jnp.bfloat16)
    two_site = two_site.reshape(rows_count, levels * levels, bond_dim)
    gated_pair = jnp.einsum(
        "xy,ayc->axc", gate_matrix, two_site, preferred_element_type=jnp.float32
    ).astype(jnp.bfloat16)
    return gated_pair.reshape(rows_count * levels, levels * bond_dim)


def basis_from(sampled, gram_matrix, left_scale):
    factor_lower = jnp.linalg.cholesky(gram_matrix)
    basis_rows = jax.scipy.linalg.solve_triangular(factor_lower, sampled.T, lower=True)
    return (basis_rows.T * left_scale).astype(jnp.bfloat16)


def apply_layer(tensor, gate_matrix, sketch_whole, parity):
    bond_dim = tensor.shape[0]
    levels = tensor.shape[1]
    left_scale = levels**0.5 * bond_dim**0.25
    right_scale = (levels * bond_dim) ** (-0.5)
    devices = lax.axis_size("site")
    position = lax.axis_index("site")
    is_left = ((position - parity) % 2 == 0) & (position + 1 < devices)
    is_right = ((position - 1 - parity) % 2 == 0) & (position >= 1)
    sketch_values = sketch_whole.astype(jnp.bfloat16)
    partner = from_behind(tensor, "site", -1)
    matrix = contract(tensor, partner, gate_matrix)
    sampled = jnp.dot(matrix, sketch_values, preferred_element_type=jnp.float32)
    gram_matrix = jnp.dot(sampled.T, sampled, precision=lax.Precision.HIGHEST)
    left_rows = basis_from(sampled, gram_matrix, left_scale)
    product = lax.dot_general(
        left_rows, matrix, (((0,), (0,)), ((), ())), preferred_element_type=jnp.float32
    )
    new_right = (product * right_scale).astype(jnp.bfloat16).reshape(bond_dim, levels, bond_dim)
    new_left = left_rows.reshape(bond_dim, levels, bond_dim)
    arrived = from_behind(new_right, "site", 1)
    return jnp.where(is_left, new_left, jnp.where(is_right, arrived, tensor))


def per_device(site_tensors, first_gates, second_gates, first_sketch, second_sketch):
    tensor = site_tensors[0]
    tensor = apply_layer(tensor, first_gates[0], first_sketch[0], 0)
    tensor = apply_layer(tensor, second_gates[0], second_sketch[0], 1)
    return tensor[None]


def solution(mesh):
    in_specs = (
        P("site", None, None, None),
        P("site", None, None),
        P("site", None, None),
        P("site", None, None),
        P("site", None, None),
    )
    out_specs = P("site", None, None, None)
    return jax.shard_map(
        per_device, mesh=mesh, in_specs=in_specs, out_specs=out_specs, check_vma=False
    )
```

profile of v0, /device:TPU:24, one launch (start us, length us, event | category | flops | bytes accessed | tf_op | source)
XLA Modules:
  0.0 323.5 jit_solution(18346635609313952229)
XLA Ops:
  0.0 3.8 %collective-permute-start = (bf16[256,8,256]{2,1,0:T(8,128)(2,1)}, bf16[256,8,256]{2,1,0:T(8,128)(2,1)S(1)}, u32[]{:S(2)}, u32[]{:S(2)}) collective-permute-start(bf16[256,8,256]{2,1,0:T(8,128)(2,1)} %bitcast.126), channel_id=1, source_target_pairs={{1,0},{2,1},{3,2},{4,3},{5,4},{6,5},{7,6},{8,7},{9,8},{10,9},{11,1... | collective-permute-start | bytes 3145736 | tf_op jit(solution)/shard_map/ppermute | solution.py:10
  3.8 12.6 %collective-permute-done = bf16[256,8,256]{2,1,0:T(8,128)(2,1)S(1)} collective-permute-done((bf16[256,8,256]{2,1,0:T(8,128)(2,1)}, bf16[256,8,256]{2,1,0:T(8,128)(2,1)S(1)}, u32[]{:S(2)}, u32[]{:S(2)}) %collective-permute-start) | collective-permute-done | bytes 1048608 | tf_op jit(solution)/shard_map/ppermute | solution.py:10
  16.7 5.6 %convolution_convert_fusion.1 = bf16[2048,2048]{1,0:T(8,128)(2,1)} fusion(bf16[256,2048]{1,0:T(8,128)(2,1)S(1)} %bitcast.127, bf16[1,256,8,256]{3,2,1,0:T(8,128)(2,1)S(1)} %copy-done.4), kind=kOutput, calls=%fused_computation.7 | convolution fusion | flops 2151677952 | bytes 10485760 | tf_op jit(solution)/shard_map/dot_general | solution.py:17
  22.3 13.5 %reshape.51 = bf16[256,64,256]{2,1,0:T(8,128)(2,1)} reshape(bf16[2048,2048]{1,0:T(8,128)(2,1)} %convolution_convert_fusion.1) | data formatting | bytes 16777216 | tf_op jit(solution)/shard_map/reshape | solution.py:22
  35.8 8.9 %convert_bitcast_fusion.1 = bf16[256,64,256]{2,1,0:T(8,128)(2,1)} fusion(bf16[256,64,256]{2,1,0:T(8,128)(2,1)} %reshape.51, bf16[1,64,64]{2,1,0:T(8,128)(2,1)S(1)} %copy-done), kind=kOutput, calls=%fused_computation.5 | convolution fusion | flops 541065216 | bytes 16785408 | tf_op jit(solution)/shard_map/xy,ayc->axc/dot_general | solution.py:23
  44.7 14.0 %reshape.52 = bf16[2048,2048]{1,0:T(8,128)(2,1)} reshape(bf16[256,64,256]{2,1,0:T(8,128)(2,1)} %convert_bitcast_fusion.1) | data formatting | bytes 16777216 | tf_op jit(solution)/shard_map/reshape | solution.py:26
  58.7 6.3 %fusion.12 = f32[2048,256]{1,0:T(8,128)S(1)} fusion(bf16[2048,2048]{1,0:T(8,128)(2,1)} %reshape.52, s32[1,2048,256]{2,1,0:T(8,128)} %param.11), kind=kOutput, calls=%fused_computation.30 | convolution fusion | flops 2148007936 | bytes 12582912 | tf_op jit(solution)/shard_map/dot_general | solution.py:47
  65.1 3.5 %fusion.45 = f32[256,256]{1,0:T(8,128)S(1)} fusion(f32[2048,256]{1,0:T(8,128)S(1)} %fusion.12), kind=kOutput, calls=%fused_computation.85 | convolution fusion | flops 1610612736 | bytes 2359296 | tf_op jit(solution)/shard_map/dot_general | solution.py:48
  68.8 11.7 %cholesky.130 = f32[128,128]{1,0:T(8,128)S(1)} custom-call(f32[128,128]{1,0:T(8,128)S(1)} %cholesky.194), custom_call_target="Cholesky" | custom-call | tf_op jit(solution)/shard_map/jit(cholesky)/cholesky | solution.py:30
  80.5 9.8 %custom-call.13 = f32[1,128,128]{1,2,0:T(8,128)S(1)} custom-call(f32[1,128,128]{2,1,0:T(8,128)S(1)} %get-tuple-element.50), custom_call_target="InvertDiagBlocksLowerTriangular" | custom-call | tf_op jit(solution)/shard_map/jit(cholesky)/cholesky | solution.py:30
  91.0 11.7 %cholesky.147 = f32[128,128]{1,0:T(8,128)S(1)} custom-call(f32[128,128]{1,0:T(8,128)S(1)} %convolution_subtract_fusion.3), custom_call_target="Cholesky" | custom-call | tf_op jit(solution)/shard_map/jit(cholesky)/cholesky | solution.py:30
  104.8 3.8 %while.4 = (s32[]{:T(128)}, f32[256,256]{1,0:T(8,128)S(1)}, s32[2,2]{1,0:T(2,128)S(1)}, f32[2,128,128]{2,1,0:T(8,128)S(1)}, s32[]{:T(128)}) while((s32[]{:T(128)}, f32[256,256]{1,0:T(8,128)S(1)}, s32[2,2]{1,0:T(2,128)S(1)}, f32[2,128,128]{2,1,0:T(8,128)S(1)}, s32[]{:T(128)}) %tuple.43), condition=%wide.while_cond, body=%wide.while_body.sunk | while | flops 2 | bytes 131181 | solution.py:31
  105.4 1.3 bitcast_dynamic-update-slice_fusion.4
  107.3 1.3 bitcast_dynamic-update-slice_fusion.4
  108.7 19.7 %custom-call.14 = f32[2,128,128]{1,2,0:T(8,128)S(1)} custom-call(f32[2,128,128]{2,1,0:T(8,128)S(1)} %get-tuple-element.21), custom_call_target="InvertDiagBlocksLowerTriangular" | custom-call | tf_op jit(solution)/shard_map/jit(_solve_triangular)/triangular_solve | solution.py:31
  128.3 1.1 fusion.6
  129.4 1.8 convolution_subtract_fusion.1
  131.3 1.1 fusion.24
  132.3 5.7 %fusion = bf16[256,2048]{1,0:T(8,128)(2,1)S(1)} fusion(bf16[2048,2048]{1,0:T(8,128)(2,1)} %reshape.52, f32[128,2048]{1,0:T(8,128)S(1)} %fusion.24, f32[128,2048]{1,0:T(8,128)S(1)} %fusion.6), kind=kOutput, calls=%fused_computation.10 | convolution fusion | flops 2150105088 | bytes 11534336 | tf_op jit(solution)/shard_map/dot_general | solution.py:50
  138.1 1.3 copy.15
  139.3 1.9 collective-permute-start.1
  141.3 1.2 fusion.36
  142.5 1.5 copy.11
  144.0 13.7 %collective-permute-done.1 = bf16[256,8,256]{2,1,0:T(8,128)(2,1)} collective-permute-done((bf16[256,8,256]{2,1,0:T(8,128)(2,1)}, bf16[256,8,256]{2,1,0:T(8,128)(2,1)}, u32[]{:S(2)}, u32[]{:S(2)}) %collective-permute-start.1) | collective-permute-done | bytes 1048608 | tf_op jit(solution)/shard_map/ppermute | solution.py:10
  157.8 2.4 collective-permute-start.2
  160.2 12.3 %collective-permute-done.2 = bf16[256,8,256]{2,1,0:T(8,128)(2,1)S(1)} collective-permute-done((bf16[256,8,256]{2,1,0:T(8,128)(2,1)S(1)}, bf16[256,8,256]{2,1,0:T(8,128)(2,1)S(1)}, u32[]{:S(2)}, u32[]{:S(2)}) %collective-permute-start.2) | collective-permute-done | bytes 1048608 | tf_op jit(solution)/shard_map/ppermute | solution.py:10
  172.8 5.6 %convolution_convert_fusion = bf16[2048,2048]{1,0:T(8,128)(2,1)} fusion(bf16[256,2048]{1,0:T(8,128)(2,1)S(1)} %bitcast.128, bf16[256,8,256]{2,1,0:T(8,128)(2,1)S(1)} %bitcast_select_fusion.1), kind=kOutput, calls=%fused_computation.6 | convolution fusion | flops 2151677952 | bytes 10485760 | tf_op jit(solution)/shard_map/dot_general | solution.py:17
  178.4 13.5 %reshape.57 = bf16[256,64,256]{2,1,0:T(8,128)(2,1)} reshape(bf16[2048,2048]{1,0:T(8,128)(2,1)} %convolution_convert_fusion) | data formatting | bytes 16777216 | tf_op jit(solution)/shard_map/reshape | solution.py:22
  191.9 8.9 %convert_bitcast_fusion = bf16[256,64,256]{2,1,0:T(8,128)(2,1)} fusion(bf16[256,64,256]{2,1,0:T(8,128)(2,1)} %reshape.57, bf16[1,64,64]{2,1,0:T(8,128)(2,1)S(1)} %copy-done.9), kind=kOutput, calls=%fused_computation.4 | convolution fusion | flops 541065216 | bytes 16785408 | tf_op jit(solution)/shard_map/xy,ayc->axc/dot_general | solution.py:23
  200.8 13.9 %reshape.58 = bf16[2048,2048]{1,0:T(8,128)(2,1)} reshape(bf16[256,64,256]{2,1,0:T(8,128)(2,1)} %convert_bitcast_fusion) | data formatting | bytes 16777216 | tf_op jit(solution)/shard_map/reshape | solution.py:26
  214.7 6.3 %fusion.9 = f32[2048,256]{1,0:T(8,128)S(1)} fusion(bf16[2048,2048]{1,0:T(8,128)(2,1)} %reshape.58, s32[1,2048,256]{2,1,0:T(8,128)} %param.12), kind=kOutput, calls=%fused_computation.26 | convolution fusion | flops 2148007936 | bytes 12582912 | tf_op jit(solution)/shard_map/dot_general | solution.py:47
  221.1 3.5 %fusion.46 = f32[256,256]{1,0:T(8,128)S(1)} fusion(f32[2048,256]{1,0:T(8,128)S(1)} %fusion.9), kind=kOutput, calls=%fused_computation.86 | convolution fusion | flops 1610612736 | bytes 2359296 | tf_op jit(solution)/shard_map/dot_general | solution.py:48
  227.1 11.7 %cholesky.164 = f32[128,128]{1,0:T(8,128)S(1)} custom-call(f32[128,128]{1,0:T(8,128)S(1)} %cholesky.197), custom_call_target="Cholesky" | custom-call | tf_op jit(solution)/shard_map/jit(cholesky)/cholesky | solution.py:30
  238.9 9.8 %custom-call.15 = f32[1,128,128]{1,2,0:T(8,128)S(1)} custom-call(f32[1,128,128]{2,1,0:T(8,128)S(1)} %get-tuple-element.46), custom_call_target="InvertDiagBlocksLowerTriangular" | custom-call | tf_op jit(solution)/shard_map/jit(cholesky)/cholesky | solution.py:30
  249.7 1.3 convolution_subtract_fusion.2
  251.0 11.7 %cholesky.181 = f32[128,128]{1,0:T(8,128)S(1)} custom-call(f32[128,128]{1,0:T(8,128)S(1)} %convolution_subtract_fusion.2), custom_call_target="Cholesky" | custom-call | tf_op jit(solution)/shard_map/jit(cholesky)/cholesky | solution.py:30
  266.3 3.8 %while.5 = (s32[]{:T(128)}, f32[256,256]{1,0:T(8,128)S(1)}, s32[2,2]{1,0:T(2,128)S(1)}, f32[2,128,128]{2,1,0:T(8,128)S(1)}, s32[]{:T(128)}) while((s32[]{:T(128)}, f32[256,256]{1,0:T(8,128)S(1)}, s32[2,2]{1,0:T(2,128)S(1)}, f32[2,128,128]{2,1,0:T(8,128)S(1)}, s32[]{:T(128)}) %tuple.49), condition=%wide.while_cond.clone, body=%wide.while_body.clone.sunk | while | flops 2 | bytes 131181 | solution.py:31
  266.9 1.3 bitcast_dynamic-update-slice_fusion.5
  268.8 1.3 bitcast_dynamic-update-slice_fusion.5
  270.8 20.7 %custom-call.16 = f32[2,128,128]{1,2,0:T(8,128)S(1)} custom-call(f32[2,128,128]{2,1,0:T(8,128)} %copy-done.8), custom_call_target="InvertDiagBlocksLowerTriangular" | custom-call | tf_op jit(solution)/shard_map/jit(_solve_triangular)/triangular_solve | solution.py:31
  292.6 1.8 convolution_subtract_fusion
  295.5 5.7 %fusion.1 = bf16[256,2048]{1,0:T(8,128)(2,1)S(1)} fusion(bf16[2048,2048]{1,0:T(8,128)(2,1)} %reshape.58, f32[128,2048]{1,0:T(8,128)S(1)} %fusion.20, f32[128,2048]{1,0:T(8,128)S(1)} %fusion.4), kind=kOutput, calls=%fused_computation.11 | convolution fusion | flops 2150105088 | bytes 11534336 | tf_op jit(solution)/shard_map/dot_general | solution.py:50
  301.2 1.3 copy.17
  302.5 1.9 collective-permute-start.3
  304.4 1.2 fusion.34
  305.6 1.5 copy.13
  307.1 13.8 %collective-permute-done.3 = bf16[256,8,256]{2,1,0:T(8,128)(2,1)} collective-permute-done((bf16[256,8,256]{2,1,0:T(8,128)(2,1)}, bf16[256,8,256]{2,1,0:T(8,128)(2,1)}, u32[]{:S(2)}, u32[]{:S(2)}) %collective-permute-start.3) | collective-permute-done | bytes 1048608 | tf_op jit(solution)/shard_map/ppermute | solution.py:10
  320.9 2.3 fusion.8
  (61 shorter events, 13.6 us)
Async XLA Ops:
  0.0 35.8 %copy-start = (bf16[1,64,64]{2,1,0:T(8,128)(2,1)S(1)}, bf16[1,64,64]{2,1,0:T(8,128)(2,1)}, u32[]{:S(2)}) copy-start(bf16[1,64,64]{2,1,0:T(8,128)(2,1)} %param.9) | copy-start | bytes 24580
  0.0 16.7 %copy-start.4 = (bf16[1,256,8,256]{3,2,1,0:T(8,128)(2,1)S(1)}, bf16[1,256,8,256]{3,2,1,0:T(8,128)(2,1)}, u32[]{:S(2)}) copy-start(bf16[1,256,8,256]{3,2,1,0:T(8,128)(2,1)} %param.8) | copy-start | bytes 3145732
  0.0 16.4 %collective-permute-start = (bf16[256,8,256]{2,1,0:T(8,128)(2,1)}, bf16[256,8,256]{2,1,0:T(8,128)(2,1)S(1)}, u32[]{:S(2)}, u32[]{:S(2)}) collective-permute-start(bf16[256,8,256]{2,1,0:T(8,128)(2,1)} %bitcast.126), channel_id=1, source_target_pairs={{1,0},{2,1},{3,2},{4,3},{5,4},{6,5},{7,6},{8,7},{9,8},{10,9},{11,1... | collective-permute-start | bytes 3145736 | tf_op jit(solution)/shard_map/ppermute | solution.py:10
  108.7 22.6 %copy-start.10 = (s32[2,2]{1,0:T(2,128)}, s32[2,2]{1,0:T(2,128)S(1)}, u32[]{:S(2)}) copy-start(s32[2,2]{1,0:T(2,128)S(1)} %get-tuple-element.151) | copy-start | bytes 52
  139.3 18.3 %collective-permute-start.1 = (bf16[256,8,256]{2,1,0:T(8,128)(2,1)}, bf16[256,8,256]{2,1,0:T(8,128)(2,1)}, u32[]{:S(2)}, u32[]{:S(2)}) collective-permute-start(bf16[256,8,256]{2,1,0:T(8,128)(2,1)} %bitcast.37), channel_id=1, source_target_pairs={{0,1},{1,2},{2,3},{3,4},{4,5},{5,6},{6,7},{7,8},{8,9},{9,10},{10,1... | collective-permute-start | bytes 3145736 | tf_op jit(solution)/shard_map/ppermute | solution.py:10
  141.3 16.3 %copy-start.5 = (bf16[1,256,8,256]{3,2,1,0:T(8,128)(2,1)S(1)}, bf16[1,256,8,256]{3,2,1,0:T(8,128)(2,1)}, u32[]{:S(2)}) copy-start(bf16[1,256,8,256]{3,2,1,0:T(8,128)(2,1)} %param.8) | copy-start | bytes 3145732
  157.8 14.7 %collective-permute-start.2 = (bf16[256,8,256]{2,1,0:T(8,128)(2,1)S(1)}, bf16[256,8,256]{2,1,0:T(8,128)(2,1)S(1)}, u32[]{:S(2)}, u32[]{:S(2)}) collective-permute-start(bf16[256,8,256]{2,1,0:T(8,128)(2,1)S(1)} %bitcast_select_fusion.1), channel_id=1, source_target_pairs={{1,0},{2,1},{3,2},{4,3},{5,4},{6,5},{7,6},{8,7},{9,8},{10,9},{11,1... | collective-permute-start | bytes 3145736 | tf_op jit(solution)/shard_map/ppermute | solution.py:10
  178.4 13.5 %copy-start.9 = (bf16[1,64,64]{2,1,0:T(8,128)(2,1)S(1)}, bf16[1,64,64]{2,1,0:T(8,128)(2,1)}, u32[]{:S(2)}) copy-start(bf16[1,64,64]{2,1,0:T(8,128)(2,1)} %param.10) | copy-start | bytes 24580
  224.5 41.8 %copy-start.11 = (s32[2,2]{1,0:T(2,128)S(1)}, s32[2,2]{1,0:T(2,128)}, u32[]{:S(2)}) copy-start(s32[2,2]{1,0:T(2,128)} %copy-done.10) | copy-start | bytes 52
  226.4 0.7 copy-start.7
  262.7 2.5 copy-start.6
  270.1 0.7 copy-start.8
  292.6 2.9 copy-start.2
  301.2 3.2 %copy-start.3 = (f32[128,2048]{1,0:T(8,128)S(1)}, f32[128,2048]{1,0:T(8,128)}, u32[]{:S(2)}) copy-start(f32[128,2048]{1,0:T(8,128)} %copy-done.2) | copy-start | bytes 3145732
  302.5 18.4 %collective-permute-start.3 = (bf16[256,8,256]{2,1,0:T(8,128)(2,1)}, bf16[256,8,256]{2,1,0:T(8,128)(2,1)}, u32[]{:S(2)}, u32[]{:S(2)}) collective-permute-start(bf16[256,8,256]{2,1,0:T(8,128)(2,1)} %bitcast.41), channel_id=1, source_target_pairs={{0,1},{1,2},{2,3},{3,4},{4,5},{5,6},{6,7},{7,8},{8,9},{9,10},{10,1... | collective-permute-start | bytes 3145736 | tf_op jit(solution)/shard_map/ppermute | solution.py:10
  305.6 17.6 %copy-start.1 = (bf16[1,64,64]{2,1,0:T(8,128)(2,1)S(1)}, bf16[1,64,64]{2,1,0:T(8,128)(2,1)}, u32[]{:S(2)}) copy-start(bf16[1,64,64]{2,1,0:T(8,128)(2,1)} %param.9) | copy-start | bytes 24580
where the time goes:
time: 330 us; the launch traced here: 323 us
  other arithmetic  116 us (35%)
  local copies, waits for them, and re-layouts  71 us (22%)
  matrix products  70.9 us (21%)
  waiting for transfers between devices  52.4 us (16%)
  starting transfers between devices  10 us (3%)
    another operation x13, other arithmetic, basis_from(): factor_lower = jnp.linalg.cholesky(gram_matrix)  68.6 us
    ppermute x4, waiting for transfers between devices, from_behind(): return lax.ppermute(array, axis, pairs)  52.4 us
    another operation x5, other arithmetic, basis_from(): jax.scipy.linalg.solve_triangular(factor_lower, sampled.T, lower=True)  41.4 us
    reshape x2, local copies, waits for them, and re-layouts, contract(): return gated_pair.reshape(rows_count * levels, levels * bond_dim)  27.9 us
    reshape x2, local copies, waits for them, and re-layouts, contract(): two_site = two_site.reshape(rows_count, levels * levels, bond_dim)  27 us
    dot_general x2, matrix products, contract(): jnp.einsum('xy,ayc->axc', gate_matrix, two_site, preferred_element_type=j...  17.9 us
    dot_general x2, matrix products, apply_layer(): sampled = jnp.dot(matrix, sketch_values, preferred_element_type=jnp.float32)  12.7 us
    dot_general x2, matrix products, apply_layer(): lax.dot_general(left_rows, matrix, (((0,), (0,)), ((), ())), preferred_el...  11.4 us
  transfers between devices with their start and end apart: 4, of which 4 were waited for; matrix products, arithmetic and copies ran while one was open for 2% of the time, Pallas kernels for 0%

commit v1 on v0

v1 whole, which is shorter than its diff:
```python
import functools

import jax
import jax.numpy as jnp
from jax import lax
from jax.experimental import pallas as pl
from jax.experimental.pallas import tpu as pltpu
from jax.sharding import PartitionSpec as P

PANEL = 32
F32 = jnp.float32
BF16 = jnp.bfloat16


def dot(a, b, dims=((1,), (0,)), precision=None):
    return lax.dot_general(a, b, (dims, ((), ())), precision=precision, preferred_element_type=F32)


def split(x, parts):
    pieces = []
    for _ in range(parts):
        piece = x.astype(BF16)
        pieces.append(piece)
        x = x - piece.astype(F32)
    return pieces


def wide_gate(gate, levels, group):
    size = levels * levels * group

    def pick(position):
        high, low = position // (group * levels), position % levels
        return low * levels + high

    rows = pick(lax.broadcasted_iota(jnp.int32, (size, levels * levels), 0))
    left = (rows == lax.broadcasted_iota(jnp.int32, (size, levels * levels), 1)).astype(F32).astype(BF16)
    columns = pick(lax.broadcasted_iota(jnp.int32, (levels * levels, size), 1))
    right = (columns == lax.broadcasted_iota(jnp.int32, (levels * levels, size), 0)).astype(F32).astype(BF16)
    spread = dot(dot(left, gate).astype(BF16), right)
    bond_of = lambda axis: (lax.broadcasted_iota(jnp.int32, (size, size), axis) // levels) % group
    return jnp.where(bond_of(0) == bond_of(1), spread, 0.0).astype(BF16)


def invert_factor(gram):
    size = gram.shape[0]
    work = gram
    done = []
    for start in range(0, size, PANEL):
        panel = work[:PANEL]
        rest = work[PANEL:]
        row_of = lax.broadcasted_iota(jnp.int32, (PANEL, 1), 0)
        lane_of = lax.broadcasted_iota(jnp.int32, (1, size), 1)
        for k in range(PANEL):
            lane = start + k
            column = panel[:, lane : lane + 1]
            root = lax.rsqrt(column[k : k + 1])
            row = jnp.where(lane_of == lane, 1.0, panel[k : k + 1]) * root
            below = row_of > k
            factor = jnp.where(below, column * root, 0.0)
            cleared = jnp.where(below & (lane_of == lane), 0.0, panel)
            panel = jnp.where(row_of == k, row, cleared - factor * row)
        done.append(panel)
        if start + PANEL < size:
            past = lane_of >= start + PANEL
            upper = jnp.where(past, panel, 0.0)
            inside = (lane_of >= start) & (lane_of < start + PANEL)
            reached = jnp.where(inside & (lane_of > start + row_of), 0.0, panel)
            update = dot(upper, reached, ((0,), (0,)), lax.Precision.HIGHEST)
            work = jnp.where(inside, 0.0, rest) - update[start + PANEL :]
    lower = jnp.concatenate(done, axis=0)
    keep = lax.broadcasted_iota(jnp.int32, (size, size), 0) >= lax.broadcasted_iota(jnp.int32, (size, size), 1)
    return jnp.where(keep, lower, 0.0)


def layer_kernel(
    parity, levels, bond,
    own, other, own_gate, other_gate, own_sketch, other_sketch, out,
    left, right, right_wide, spread, gate, wide, sketch, matrix, sampled, gram, basis_t, sems,
):
    devices = lax.axis_size("site")
    position = lax.axis_index("site")
    is_left = ((position - parity) % 2 == 0) & (position >= parity) & (position + 1 < devices)
    is_right = ((position - parity) % 2 != 0) & (position > parity)
    rows = bond * levels
    group = wide.shape[0] // (levels * levels)
    height = group * levels
    chunk = bond
    left_scale = levels**0.5 * bond**0.25
    right_scale = rows**-0.5

    def fetch(pairs):
        copies = [pltpu.make_async_copy(a, b, sems.at[i]) for i, (a, b) in enumerate(pairs)]
        for copy in copies:
            copy.start()
        for copy in copies:
            copy.wait()

    @pl.when(is_left)
    def _():
        fetch([(own, left), (other, right), (own_gate, gate), (own_sketch, sketch)])

    @pl.when(is_right)
    def _():
        fetch([(other, left), (own, right), (other_gate, gate), (other_sketch, sketch)])

    @pl.when(jnp.logical_not(is_left | is_right))
    def _():
        fetch([(own, out)])

    @pl.when(is_left | is_right)
    def _():
        wide[...] = wide_gate(gate[...], levels, group)
        spread[...] = right[...].astype(F32).reshape(bond, levels, bond)
        for s in range(levels):
            right_wide[:, s * bond : (s + 1) * bond] = spread[:, s, :].astype(BF16)
        gram[...] = jnp.zeros_like(gram)

        @pl.loop(0, rows // chunk)
        def _(step):
            base = pl.multiple_of(step * chunk, chunk)
            two_site = dot(left[pl.ds(base, chunk), :], right_wide[...]).astype(BF16)
            for g in range(chunk // height):
                part = two_site[g * height : (g + 1) * height]
                stacked = jnp.concatenate([part[:, s * bond : (s + 1) * bond] for s in range(levels)], axis=0)
                gated = dot(wide[...], stacked).astype(BF16)
                at = pl.multiple_of(base + g * height, height)
                for t in range(levels):
                    matrix[pl.ds(at, height), t * bond : (t + 1) * bond] = gated[t * height : (t + 1) * height]
            drawn = dot(matrix[pl.ds(base, chunk), :], sketch[...])
            sampled[pl.ds(base, chunk), :] = drawn
            high, middle, low = split(drawn, 3)
            cross = dot(high, middle, ((0,), (0,))) + dot(high, low, ((0,), (0,)))
            square = dot(high, high, ((0,), (0,))) + dot(middle, middle, ((0,), (0,)))
            gram[...] += square + (cross + cross.T)

        inverse = invert_factor(gram[...])
        inv_high, inv_low = split(inverse.T * left_scale, 2)

        def basis_at(base):
            high, low = split(sampled[pl.ds(base, chunk), :], 2)
            return dot(high, inv_high) + (dot(high, inv_low) + dot(low, inv_high))

        @pl.when(is_left)
        def _():
            for step in range(rows // chunk):
                out[step * chunk : (step + 1) * chunk, :] = basis_at(step * chunk).astype(BF16)

        @pl.when(is_right)
        def _():
            for step in range(rows // chunk):
                basis_t[:, step * chunk : (step + 1) * chunk] = basis_at(step * chunk).T.astype(BF16)
            for t in range(levels):
                product = dot(basis_t[...], matrix[:, t * bond : (t + 1) * bond])
                spread[:, t, :] = product * right_scale
            out[...] = spread[...].reshape(rows, bond).astype(BF16)


def apply_layer(parity, own, other, own_gate, other_gate, own_sketch, other_sketch):
    bond, levels = own_sketch.shape[1], own.shape[0] // own_sketch.shape[1]
    rows = bond * levels
    group = max(1, bond // (levels * levels))
    size = group * levels * levels
    return pl.pallas_call(
        functools.partial(layer_kernel, parity, levels, bond),
        out_shape=jax.ShapeDtypeStruct((rows, bond), BF16),
        in_specs=[pl.BlockSpec(memory_space=pl.ANY)] * 6,
        out_specs=pl.BlockSpec(memory_space=pltpu.VMEM),
        scratch_shapes=[
            pltpu.VMEM((rows, bond), BF16),
            pltpu.VMEM((rows, bond), BF16),
            pltpu.VMEM((bond, rows), BF16),
            pltpu.VMEM((bond, levels, bond), F32),
            pltpu.VMEM(own_gate.shape, BF16),
            pltpu.VMEM((size, size), BF16),
            pltpu.VMEM((rows, bond), BF16),
            pltpu.VMEM((rows, rows), BF16),
            pltpu.VMEM((rows, bond), F32),
            pltpu.VMEM((bond, bond), F32),
            pltpu.VMEM((bond, rows), BF16),
            pltpu.SemaphoreType.DMA((4,)),
        ],
        compiler_params=pltpu.CompilerParams(vmem_limit_bytes=48 * 1024 * 1024),
        cost_estimate=pl.CostEstimate(flops=8 * rows * rows * bond, bytes_accessed=8 * rows * bond, transcendentals=0),
    )(own, other, own_gate, other_gate, own_sketch, other_sketch)


def per_device(site_tensors, first_gates, second_gates, first_sketch, second_sketch):
    size = lax.axis_size("site")
    _, bond, levels, _ = site_tensors.shape
    tensor = site_tensors.reshape(bond * levels, bond)
    arguments = [
        (0, first_gates[0], first_sketch[0].astype(BF16)),
        (1, second_gates[0], second_sketch[0].astype(BF16)),
    ]
    sent = []
    for parity, gate, sketch in arguments:
        to_right = [(i, i + 1) for i in range(parity, size - 1, 2)]
        sent.append((lax.ppermute(gate, "site", to_right), lax.ppermute(sketch, "site", to_right)))
    for (parity, gate, sketch), (other_gate, other_sketch) in zip(arguments, sent):
        swaps = [pair for i in range(parity, size - 1, 2) for pair in ((i, i + 1), (i + 1, i))]
        other = lax.ppermute(tensor, "site", swaps)
        tensor = apply_layer(parity, tensor, other, gate, other_gate, sketch, other_sketch)
    return tensor.reshape(site_tensors.shape)


def solution(mesh):
    in_specs = (
        P("site", None, None, None),
        P("site", None, None),
        P("site", None, None),
        P("site", None, None),
        P("site", None, None),
    )
    out_specs = P("site", None, None, None)
    return jax.shard_map(
        per_device, mesh=mesh, in_specs=in_specs, out_specs=out_specs, check_vma=False
    )
```

time: 330 us -> 137 us (0.42)
  the two profiles are of different devices: /device:TPU:24 before, /device:TPU:4 now
where the time goes in v1:
time: 137 us; the launch traced here: 136 us
  Pallas kernels  95.5 us (70%)
  waiting for transfers between devices  22 us (16%)
  starting transfers between devices  14.9 us (11%)
  other arithmetic  3.61 us (3%)
    pallas_call x2, Pallas kernels, apply_layer(): pl.pallas_call(functools.partial(layer_kernel, parity, levels, bond), out...  95.5 us
    ppermute x2, waiting for transfers between devices, per_device(): lax.ppermute(gate, 'site', to_right)  22 us
    ppermute x2, starting transfers between devices, per_device(): other = lax.ppermute(tensor, 'site', swaps)  8.14 us
    ppermute x2, starting transfers between devices, per_device(): lax.ppermute(gate, 'site', to_right)  3.67 us
    ppermute x2, starting transfers between devices, per_device(): lax.ppermute(sketch, 'site', to_right)  3.1 us
  transfers between devices with their start and end apart: 6, of which 1 were waited for; matrix products, arithmetic and copies ran while one was open for 1% of the time, Pallas kernels for 34%

profile of v1, /device:TPU:4, one launch (start us, length us, event | category | flops | bytes accessed | tf_op | source)
XLA Modules:
  0.0 136.3 jit_solution(10895516474662906294)
XLA Ops:
  0.0 0.0 copy-start
  0.0 0.0 copy-start.1
  0.0 1.8 %convert_bitcast_fusion.1.own_sketch = bf16[2048,256]{1,0:T(8,128)(2,1)S(1)} fusion(s32[1,2048,256]{2,1,0:T(8,128)} %param.8), kind=kLoop, calls=%fused_computation.1 | loop fusion | flops 524288 | bytes 3145728 | tf_op jit(solution)/shard_map/convert_element_type | solution.py:192
  1.9 1.8 %collective-permute-start.2 = (bf16[2048,256]{1,0:T(8,128)(2,1)S(1)}, bf16[2048,256]{1,0:T(8,128)(2,1)S(1)}, u32[]{:S(2)}, u32[]{:S(2)}) collective-permute-start(bf16[2048,256]{1,0:T(8,128)(2,1)S(1)} %convert_bitcast_fusion.1.own_sketch), channel_id=1, source_target_pairs={{0,1},{2,3},{4,5},{6,7},{8,9},{10,11},{12,13},{14,15},{16,17},{18,... | collective-permute-start | bytes 3145736 | tf_op jit(solution)/shard_map/ppermute | solution.py:198
  3.7 0.0 copy-done
  3.7 0.1 collective-permute-start
  3.8 0.0 copy-done.1
  3.8 2.4 %collective-permute-start.1 = (bf16[64,64]{1,0:T(8,128)(2,1)S(1)}, bf16[64,64]{1,0:T(8,128)(2,1)S(1)}, u32[]{:S(2)}, u32[]{:S(2)}) collective-permute-start(bf16[64,64]{1,0:T(8,128)(2,1)S(1)} %bitcast.10), channel_id=1, source_target_pairs={{0,1},{2,3},{4,5},{6,7},{8,9},{10,11},{12,13},{14,15},{16,17},{18,... | collective-permute-start | bytes 24584 | tf_op jit(solution)/shard_map/ppermute | solution.py:198
  6.2 1.8 %convert_bitcast_fusion.own_sketch = bf16[2048,256]{1,0:T(8,128)(2,1)S(1)} fusion(s32[1,2048,256]{2,1,0:T(8,128)} %param.9), kind=kLoop, calls=%fused_computation | loop fusion | flops 524288 | bytes 3145728 | tf_op jit(solution)/shard_map/convert_element_type | solution.py:193
  7.9 0.0 copy-start.2
  7.9 1.3 collective-permute-start.5
  9.2 0.0 collective-permute-done.1.other_gate
  9.2 0.0 collective-permute-done.2.other_sketch
  9.3 0.0 collective-permute-done.other
  9.3 45.8 %shard_map.55.own = bf16[2048,256]{1,0:T(8,128)(2,1)S(1)} custom-call(bf16[2048,256]{1,0:T(8,128)(2,1)S(1)} %bitcast.9, bf16[2048,256]{1,0:T(8,128)(2,1)S(1)} %collective-permute-done.other, bf16[64,64]{1,0:T(8,128)(2,1)S(1)} %bitcast.11, bf16[64,64]{1,0:T(8,128)(2,1)S(1)} %collective-permute-done.1.other_gate, ...), custom_call_target="tpu_custom_call" | custom-call | flops 8589934592 | bytes 4194304 | tf_op jit(solution)/shard_map/pallas_call | solution.py:163
  55.0 8.1 %collective-permute-start.3 = (bf16[2048,256]{1,0:T(8,128)(2,1)S(1)}, bf16[2048,256]{1,0:T(8,128)(2,1)S(1)}, u32[]{:S(2)}, u32[]{:S(2)}) collective-permute-start(bf16[2048,256]{1,0:T(8,128)(2,1)S(1)} %shard_map.55.own), channel_id=1, source_target_pairs={{1,2},{2,1},{3,4},{4,3},{5,6},{6,5},{7,8},{8,7},{9,10},{10,9},{11,... | collective-permute-start | bytes 3145736 | tf_op jit(solution)/shard_map/ppermute | solution.py:201
  63.1 0.0 copy-done.2
  63.1 1.3 collective-permute-start.4
  64.4 21.9 %collective-permute-done.4.other_gate = bf16[64,64]{1,0:T(8,128)(2,1)S(1)} collective-permute-done((bf16[64,64]{1,0:T(8,128)(2,1)S(1)}, bf16[64,64]{1,0:T(8,128)(2,1)S(1)}, u32[]{:S(2)}, u32[]{:S(2)}) %collective-permute-start.4) | collective-permute-done | bytes 8224 | tf_op jit(solution)/shard_map/ppermute | solution.py:198
  86.4 0.0 collective-permute-done.5.other_sketch
  86.4 0.0 collective-permute-done.3.other
  86.4 49.7 %shard_map.56 = bf16[2048,256]{1,0:T(8,128)(2,1)} custom-call(bf16[2048,256]{1,0:T(8,128)(2,1)S(1)} %shard_map.55.own, bf16[2048,256]{1,0:T(8,128)(2,1)S(1)} %collective-permute-done.3.other, bf16[64,64]{1,0:T(8,128)(2,1)S(1)} %bitcast.13, bf16[64,64]{1,0:T(8,128)(2,1)S(1)} %collective-permute-done.4.other_gate, ...), custom_call_target="tpu_custom_call" | custom-call | flops 8589934592 | bytes 4194304 | tf_op jit(solution)/shard_map/pallas_call | solution.py:163
Async XLA Ops:
  0.0 3.7 %copy-start = (bf16[1,256,8,256]{3,2,1,0:T(8,128)(2,1)S(1)}, bf16[1,256,8,256]{3,2,1,0:T(8,128)(2,1)}, u32[]{:S(2)}) copy-start(bf16[1,256,8,256]{3,2,1,0:T(8,128)(2,1)} %param.5) | copy-start | bytes 3145732
  0.0 3.8 %copy-start.1 = (bf16[1,64,64]{2,1,0:T(8,128)(2,1)S(1)}, bf16[1,64,64]{2,1,0:T(8,128)(2,1)}, u32[]{:S(2)}) copy-start(bf16[1,64,64]{2,1,0:T(8,128)(2,1)} %param.6) | copy-start | bytes 24580
  1.9 7.4 %collective-permute-start.2 = (bf16[2048,256]{1,0:T(8,128)(2,1)S(1)}, bf16[2048,256]{1,0:T(8,128)(2,1)S(1)}, u32[]{:S(2)}, u32[]{:S(2)}) collective-permute-start(bf16[2048,256]{1,0:T(8,128)(2,1)S(1)} %convert_bitcast_fusion.1.own_sketch), channel_id=1, source_target_pairs={{0,1},{2,3},{4,5},{6,7},{8,9},{10,11},{12,13},{14,15},{16,17},{18,... | collective-permute-start | bytes 3145736 | tf_op jit(solution)/shard_map/ppermute | solution.py:198
  3.7 5.6 %collective-permute-start = (bf16[2048,256]{1,0:T(8,128)(2,1)S(1)}, bf16[2048,256]{1,0:T(8,128)(2,1)S(1)}, u32[]{:S(2)}, u32[]{:S(2)}) collective-permute-start(bf16[2048,256]{1,0:T(8,128)(2,1)S(1)} %bitcast.8), channel_id=1, source_target_pairs={{0,1},{1,0},{2,3},{3,2},{4,5},{5,4},{6,7},{7,6},{8,9},{9,8},{10,11... | collective-permute-start | bytes 3145736 | tf_op jit(solution)/shard_map/ppermute | solution.py:201
  3.8 5.5 %collective-permute-start.1 = (bf16[64,64]{1,0:T(8,128)(2,1)S(1)}, bf16[64,64]{1,0:T(8,128)(2,1)S(1)}, u32[]{:S(2)}, u32[]{:S(2)}) collective-permute-start(bf16[64,64]{1,0:T(8,128)(2,1)S(1)} %bitcast.10), channel_id=1, source_target_pairs={{0,1},{2,3},{4,5},{6,7},{8,9},{10,11},{12,13},{14,15},{16,17},{18,... | collective-permute-start | bytes 24584 | tf_op jit(solution)/shard_map/ppermute | solution.py:198
  7.9 55.2 %copy-start.2 = (bf16[1,64,64]{2,1,0:T(8,128)(2,1)S(1)}, bf16[1,64,64]{2,1,0:T(8,128)(2,1)}, u32[]{:S(2)}) copy-start(bf16[1,64,64]{2,1,0:T(8,128)(2,1)} %param.7) | copy-start | bytes 24580
  7.9 78.5 %collective-permute-start.5 = (bf16[2048,256]{1,0:T(8,128)(2,1)S(1)}, bf16[2048,256]{1,0:T(8,128)(2,1)S(1)}, u32[]{:S(2)}, u32[]{:S(2)}) collective-permute-start(bf16[2048,256]{1,0:T(8,128)(2,1)S(1)} %convert_bitcast_fusion.own_sketch), channel_id=1, source_target_pairs={{1,2},{3,4},{5,6},{7,8},{9,10},{11,12},{13,14},{15,16},{17,18},{19... | collective-permute-start | bytes 3145736 | tf_op jit(solution)/shard_map/ppermute | solution.py:198
  55.0 31.3 %collective-permute-start.3 = (bf16[2048,256]{1,0:T(8,128)(2,1)S(1)}, bf16[2048,256]{1,0:T(8,128)(2,1)S(1)}, u32[]{:S(2)}, u32[]{:S(2)}) collective-permute-start(bf16[2048,256]{1,0:T(8,128)(2,1)S(1)} %shard_map.55.own), channel_id=1, source_target_pairs={{1,2},{2,1},{3,4},{4,3},{5,6},{6,5},{7,8},{8,7},{9,10},{10,9},{11,... | collective-permute-start | bytes 3145736 | tf_op jit(solution)/shard_map/ppermute | solution.py:201
  63.1 23.2 %collective-permute-start.4 = (bf16[64,64]{1,0:T(8,128)(2,1)S(1)}, bf16[64,64]{1,0:T(8,128)(2,1)S(1)}, u32[]{:S(2)}, u32[]{:S(2)}) collective-permute-start(bf16[64,64]{1,0:T(8,128)(2,1)S(1)} %bitcast.12), channel_id=1, source_target_pairs={{1,2},{3,4},{5,6},{7,8},{9,10},{11,12},{13,14},{15,16},{17,18},{19... | collective-permute-start | bytes 24584 | tf_op jit(solution)/shard_map/ppermute | solution.py:198

commit v2 on v1

--- a/solution.py
+++ b/solution.py
@@ -8,6 +8,7 @@
 from jax.sharding import PartitionSpec as P
 
 PANEL = 32
+TILE = 8
 F32 = jnp.float32
 BF16 = jnp.bfloat16
 
@@ -41,32 +42,66 @@
     return jnp.where(bond_of(0) == bond_of(1), spread, 0.0).astype(BF16)
 
 
+def eliminate_tile(tiles, first, lane, lane_of):
+    size = tiles[first].shape[1]
+    width = min(size, 128)
+    shape = (TILE, width)
+    columns = [
+        [jnp.broadcast_to(tile[:, lane + j : lane + j + 1], shape) for j in range(TILE)] for tile in tiles[first:]
+    ]
+    pivot = columns[0]
+    entry = {(i, j): jnp.broadcast_to(pivot[j][i : i + 1], shape) for j in range(TILE) for i in range(j, TILE)}
+    here = (lane_of >= lane) & (lane_of < lane + TILE)
+    rows = []
+    for j in range(TILE):
+        row = jnp.broadcast_to(tiles[first][j : j + 1], (TILE, size))
+        rows.append(jnp.where(here, jnp.where(lane_of == lane + j, 1.0, 0.0), row))
+    repeat = lambda x: jnp.concatenate([x] * (size // width), axis=1)
+    for j in range(TILE):
+        root = lax.rsqrt(entry[j, j])
+        for i in range(j + 1, TILE):
+            entry[i, j] = entry[i, j] * root
+        for m in range(j + 1, TILE):
+            for i in range(m, TILE):
+                entry[i, m] = entry[i, m] - entry[i, j] * entry[m, j]
+        rows[j] = rows[j] * repeat(root)
+        for below in columns[1:]:
+            below[j] = below[j] * root
+        for m in range(j + 1, TILE):
+            rows[m] = rows[m] - repeat(entry[m, j]) * rows[j]
+            for below in columns[1:]:
+                below[m] = below[m] - entry[m, j] * below[j]
+    row_of = lax.broadcasted_iota(jnp.int32, (TILE, 1), 0)
+    whole = rows[0]
+    for j in range(1, TILE):
+        whole = jnp.where(row_of == j, rows[j], whole)
+    result = tiles[:first] + [whole]
+    for tile, below in zip(tiles[first + 1 :], columns[1:]):
+        terms = [repeat(below[j]) * rows[j] for j in range(TILE)]
+        while len(terms) > 1:
+            terms = [a + b for a, b in zip(terms[::2], terms[1::2])]
+        result.append(jnp.where(here, 0.0, tile) - terms[0])
+    return result
+
+
 def invert_factor(gram):
     size = gram.shape[0]
     work = gram
     done = []
+    row_of = lax.broadcasted_iota(jnp.int32, (PANEL, 1), 0)
+    lane_of = lax.broadcasted_iota(jnp.int32, (1, size), 1)
     for start in range(0, size, PANEL):
-        panel = work[:PANEL]
-        rest = work[PANEL:]
-        row_of = lax.broadcasted_iota(jnp.int32, (PANEL, 1), 0)
-        lane_of = lax.broadcasted_iota(jnp.int32, (1, size), 1)
-        for k in range(PANEL):
-            lane = start + k
-            column = panel[:, lane : lane + 1]
-            root = lax.rsqrt(column[k : k + 1])
-            row = jnp.where(lane_of == lane, 1.0, panel[k : k + 1]) * root
-            below = row_of > k
-            factor = jnp.where(below, column * root, 0.0)
-            cleared = jnp.where(below & (lane_of == lane), 0.0, panel)
-            panel = jnp.where(row_of == k, row, cleared - factor * row)
+        tiles = [work[i : i + TILE] for i in range(0, PANEL, TILE)]
+        for first in range(PANEL // TILE):
+            tiles = eliminate_tile(tiles, first, start + first * TILE, lane_of)
+        panel = jnp.concatenate(tiles, axis=0)
         done.append(panel)
         if start + PANEL < size:
-            past = lane_of >= start + PANEL
-            upper = jnp.where(past, panel, 0.0)
+            upper = jnp.where(lane_of >= start + PANEL, panel, 0.0)
             inside = (lane_of >= start) & (lane_of < start + PANEL)
             reached = jnp.where(inside & (lane_of > start + row_of), 0.0, panel)
             update = dot(upper, reached, ((0,), (0,)), lax.Precision.HIGHEST)
-            work = jnp.where(inside, 0.0, rest) - update[start + PANEL :]
+            work = jnp.where(inside, 0.0, work[PANEL:]) - update[start + PANEL :]
     lower = jnp.concatenate(done, axis=0)
     keep = lax.broadcasted_iota(jnp.int32, (size, size), 0) >= lax.broadcasted_iota(jnp.int32, (size, size), 1)
     return jnp.where(keep, lower, 0.0)
@@ -74,7 +109,7 @@
 
 def layer_kernel(
     parity, levels, bond,
-    own, other, own_gate, other_gate, own_sketch, other_sketch, out,
+    own, other, own_packed, other_packed, out,
     left, right, right_wide, spread, gate, wide, sketch, matrix, sampled, gram, basis_t, sems,
 ):
     devices = lax.axis_size("site")
@@ -95,13 +130,16 @@
         for copy in copies:
             copy.wait()
 
+    def unpack(packed):
+        return [(packed.at[0:rows], sketch), (packed.at[rows : rows + gate.shape[0]], gate)]
+
     @pl.when(is_left)
     def _():
-        fetch([(own, left), (other, right), (own_gate, gate), (own_sketch, sketch)])
+        fetch([(own, left), (other, right)] + unpack(own_packed))
 
     @pl.when(is_right)
     def _():
-        fetch([(other, left), (own, right), (other_gate, gate), (other_sketch, sketch)])
+        fetch([(other, left), (own, right)] + unpack(other_packed))
 
     @pl.when(jnp.logical_not(is_left | is_right))
     def _():
@@ -109,7 +147,7 @@
 
     @pl.when(is_left | is_right)
     def _():
-        wide[...] = wide_gate(gate[...], levels, group)
+        wide[...] = wide_gate(gate[:, : levels * levels], levels, group)
         spread[...] = right[...].astype(F32).reshape(bond, levels, bond)
         for s in range(levels):
             right_wide[:, s * bond : (s + 1) * bond] = spread[:, s, :].astype(BF16)
@@ -155,22 +193,22 @@
             out[...] = spread[...].reshape(rows, bond).astype(BF16)
 
 
-def apply_layer(parity, own, other, own_gate, other_gate, own_sketch, other_sketch):
-    bond, levels = own_sketch.shape[1], own.shape[0] // own_sketch.shape[1]
+def apply_layer(parity, own, other, own_packed, other_packed):
+    bond, levels = own.shape[1], own.shape[0] // own.shape[1]
     rows = bond * levels
     group = max(1, bond // (levels * levels))
     size = group * levels * levels
     return pl.pallas_call(
         functools.partial(layer_kernel, parity, levels, bond),
         out_shape=jax.ShapeDtypeStruct((rows, bond), BF16),
-        in_specs=[pl.BlockSpec(memory_space=pl.ANY)] * 6,
+        in_specs=[pl.BlockSpec(memory_space=pl.ANY)] * 4,
         out_specs=pl.BlockSpec(memory_space=pltpu.VMEM),
         scratch_shapes=[
             pltpu.VMEM((rows, bond), BF16),
             pltpu.VMEM((rows, bond), BF16),
             pltpu.VMEM((bond, rows), BF16),
             pltpu.VMEM((bond, levels, bond), F32),
-            pltpu.VMEM(own_gate.shape, BF16),
+            pltpu.VMEM((levels * levels, bond), BF16),
             pltpu.VMEM((size, size), BF16),
             pltpu.VMEM((rows, bond), BF16),
             pltpu.VMEM((rows, rows), BF16),
@@ -181,25 +219,25 @@
         ],
         compiler_params=pltpu.CompilerParams(vmem_limit_bytes=48 * 1024 * 1024),
         cost_estimate=pl.CostEstimate(flops=8 * rows * rows * bond, bytes_accessed=8 * rows * bond, transcendentals=0),
-    )(own, other, own_gate, other_gate, own_sketch, other_sketch)
+    )(own, other, own_packed, other_packed)
 
 
 def per_device(site_tensors, first_gates, second_gates, first_sketch, second_sketch):
     size = lax.axis_size("site")
     _, bond, levels, _ = site_tensors.shape
     tensor = site_tensors.reshape(bond * levels, bond)
-    arguments = [
-        (0, first_gates[0], first_sketch[0].astype(BF16)),
-        (1, second_gates[0], second_sketch[0].astype(BF16)),
-    ]
+    packs = []
+    for gate, sketch in ((first_gates[0], first_sketch[0]), (second_gates[0], second_sketch[0])):
+        padded = jnp.pad(gate, ((0, 0), (0, bond - gate.shape[1])))
+        packs.append(jnp.concatenate([sketch.astype(BF16), padded], axis=0))
     sent = []
-    for parity, gate, sketch in arguments:
+    for parity, packed in enumerate(packs):
         to_right = [(i, i + 1) for i in range(parity, size - 1, 2)]
-        sent.append((lax.ppermute(gate, "site", to_right), lax.ppermute(sketch, "site", to_right)))
-    for (parity, gate, sketch), (other_gate, other_sketch) in zip(arguments, sent):
+        sent.append(lax.ppermute(packed, "site", to_right))
+    for parity, packed in enumerate(packs):
         swaps = [pair for i in range(parity, size - 1, 2) for pair in ((i, i + 1), (i + 1, i))]
         other = lax.ppermute(tensor, "site", swaps)
-        tensor = apply_layer(parity, tensor, other, gate, other_gate, sketch, other_sketch)
+        tensor = apply_layer(parity, tensor, other, packed, sent[parity])
     return tensor.reshape(site_tensors.shape)
 
 

time: 137 us -> 104 us (0.76)
  Pallas kernels: 95.5 us -> 66.7 us
  starting transfers between devices: 14.9 us -> 9.33 us
  waiting for transfers between devices: 22 us -> 25.1 us
  other arithmetic: 3.61 us -> 2.23 us
    pallas_call x2, Pallas kernels: 95.5 us -> 66.7 us  [apply_layer(): pl.pallas_call(functools.partial(layer_kernel, parity, levels, bond), out...]
    ppermute x2, waiting for transfers between devices: 0.01 us -> 25.1 us  [per_device(): other = lax.ppermute(tensor, 'site', swaps)]
    ppermute x4 -> x2, waiting for transfers between devices: 22 us -> 0.01 us  [per_device(): sent.append(lax.ppermute(packed, 'site', to_right))]
    ppermute x4 -> x2, starting transfers between devices: 6.77 us -> 3.1 us  [per_device(): sent.append(lax.ppermute(packed, 'site', to_right))]
    ppermute x2, starting transfers between devices: 8.14 us -> 6.23 us  [per_device(): other = lax.ppermute(tensor, 'site', swaps)]
    convert_element_type x2, other arithmetic: 3.61 us -> 2.08 us  [per_device(): packs.append(jnp.concatenate([sketch.astype(BF16), padded], axis=0))]
  transfers between devices with their start and end apart: 6 -> 4, of which waited for: 1 -> 2; matrix products, arithmetic and copies ran while one was open for 1% -> 0% of each run, Pallas kernels for 34% -> 30%
where the time goes in v2:
time: 104 us
  Pallas kernels  66.7 us (64%)
  waiting for transfers between devices  25.1 us (24%)
  starting transfers between devices  9.33 us (9%)
  other arithmetic  2.23 us (2%)
    pallas_call x2, Pallas kernels, apply_layer(): pl.pallas_call(functools.partial(layer_kernel, parity, levels, bond), out...  66.7 us
    ppermute x2, waiting for transfers between devices, per_device(): other = lax.ppermute(tensor, 'site', swaps)  25.1 us
    ppermute x2, starting transfers between devices, per_device(): other = lax.ppermute(tensor, 'site', swaps)  6.23 us
    ppermute x2, starting transfers between devices, per_device(): sent.append(lax.ppermute(packed, 'site', to_right))  3.1 us
    convert_element_type x2, other arithmetic, per_device(): packs.append(jnp.concatenate([sketch.astype(BF16), padded], axis=0))  2.08 us
  transfers between devices with their start and end apart: 4, of which 2 were waited for; matrix products, arithmetic and copies ran while one was open for 0% of the time, Pallas kernels for 30%

profile of v2, /device:TPU:4, one launch (start us, length us, event | category | flops | bytes accessed | tf_op | source)
XLA Modules:
  0.0 103.8 jit_solution(18369551037302596528)
XLA Ops:
  0.0 0.0 copy-start.2
  0.0 0.0 copy-start
  0.0 0.0 copy-start.1
  0.0 1.9 %convert_bitcast_fusion.1 = bf16[2048,256]{1,0:T(8,128)(2,1)S(1)} fusion(s32[1,2048,256]{2,1,0:T(8,128)} %param.8), kind=kLoop, calls=%fused_computation.6 | loop fusion | flops 524288 | bytes 3145728 | tf_op jit(solution)/shard_map/convert_element_type | solution.py:232
  1.9 0.0 copy-done.2
  1.9 0.1 fusion.2.own_packed
  2.0 0.0 copy-start.3
  2.0 1.8 %collective-permute-start.1 = (bf16[2112,256]{1,0:T(8,128)(2,1)S(1)}, bf16[2112,256]{1,0:T(8,128)(2,1)S(1)}, u32[]{:S(2)}, u32[]{:S(2)}) collective-permute-start(bf16[2112,256]{1,0:T(8,128)(2,1)S(1)} %fusion.2.own_packed), channel_id=1, source_target_pairs={{0,1},{2,3},{4,5},{6,7},{8,9},{10,11},{12,13},{14,15},{16,17},{18,... | collective-permute-start | bytes 3244040 | tf_op jit(solution)/shard_map/ppermute | solution.py:236
  3.8 0.0 copy-done
  3.9 0.1 collective-permute-start
  3.9 0.0 copy-done.1
  3.9 0.2 convert_bitcast_fusion
  4.1 0.0 copy-done.3
  4.1 0.1 fusion.3.own_packed
  4.2 1.3 %collective-permute-start.3 = (bf16[2112,256]{1,0:T(8,128)(2,1)S(1)}, bf16[2112,256]{1,0:T(8,128)(2,1)S(1)}, u32[]{:S(2)}, u32[]{:S(2)}) collective-permute-start(bf16[2112,256]{1,0:T(8,128)(2,1)S(1)} %fusion.3.own_packed), channel_id=1, source_target_pairs={{1,2},{3,4},{5,6},{7,8},{9,10},{11,12},{13,14},{15,16},{17,18},{19... | collective-permute-start | bytes 3244040 | tf_op jit(solution)/shard_map/ppermute | solution.py:236
  5.5 2.1 %collective-permute-done.other = bf16[2048,256]{1,0:T(8,128)(2,1)S(1)} collective-permute-done((bf16[2048,256]{1,0:T(8,128)(2,1)S(1)}, bf16[2048,256]{1,0:T(8,128)(2,1)S(1)}, u32[]{:S(2)}, u32[]{:S(2)}) %collective-permute-start) | collective-permute-done | bytes 1048608 | tf_op jit(solution)/shard_map/ppermute | solution.py:239
  7.6 0.0 collective-permute-done.1.other_packed
  7.6 31.4 %shard_map.55.own = bf16[2048,256]{1,0:T(8,128)(2,1)S(1)} custom-call(bf16[2048,256]{1,0:T(8,128)(2,1)S(1)} %bitcast.9, bf16[2048,256]{1,0:T(8,128)(2,1)S(1)} %collective-permute-done.other, bf16[2112,256]{1,0:T(8,128)(2,1)S(1)} %fusion.2.own_packed, bf16[2112,256]{1,0:T(8,128)(2,1)S(1)} %collective-permute-done.1.other_packed), custom_call_target="tpu_custom_call" | custom-call | flops 8589934592 | bytes 4194304 | tf_op jit(solution)/shard_map/pallas_call | solution.py:201
  39.0 6.2 %collective-permute-start.2 = (bf16[2048,256]{1,0:T(8,128)(2,1)S(1)}, bf16[2048,256]{1,0:T(8,128)(2,1)S(1)}, u32[]{:S(2)}, u32[]{:S(2)}) collective-permute-start(bf16[2048,256]{1,0:T(8,128)(2,1)S(1)} %shard_map.55.own), channel_id=1, source_target_pairs={{1,2},{2,1},{3,4},{4,3},{5,6},{6,5},{7,8},{8,7},{9,10},{10,9},{11,... | collective-permute-start | bytes 3145736 | tf_op jit(solution)/shard_map/ppermute | solution.py:239
  45.2 0.0 collective-permute-done.3.other_packed
  45.2 23.0 %collective-permute-done.2.other = bf16[2048,256]{1,0:T(8,128)(2,1)S(1)} collective-permute-done((bf16[2048,256]{1,0:T(8,128)(2,1)S(1)}, bf16[2048,256]{1,0:T(8,128)(2,1)S(1)}, u32[]{:S(2)}, u32[]{:S(2)}) %collective-permute-start.2) | collective-permute-done | bytes 1048608 | tf_op jit(solution)/shard_map/ppermute | solution.py:239
  68.2 35.3 %shard_map.56 = bf16[2048,256]{1,0:T(8,128)(2,1)} custom-call(bf16[2048,256]{1,0:T(8,128)(2,1)S(1)} %shard_map.55.own, bf16[2048,256]{1,0:T(8,128)(2,1)S(1)} %collective-permute-done.2.other, bf16[2112,256]{1,0:T(8,128)(2,1)S(1)} %fusion.3.own_packed, bf16[2112,256]{1,0:T(8,128)(2,1)S(1)} %collective-permute-done.3.other_packed), custom_call_target="tpu_custom_call" | custom-call | flops 8589934592 | bytes 4194304 | tf_op jit(solution)/shard_map/pallas_call | solution.py:201
Async XLA Ops:
  0.0 1.9 %copy-start.2 = (bf16[1,64,64]{2,1,0:T(8,128)(2,1)S(1)}, bf16[1,64,64]{2,1,0:T(8,128)(2,1)}, u32[]{:S(2)}) copy-start(bf16[1,64,64]{2,1,0:T(8,128)(2,1)} %param.6) | copy-start | bytes 24580
  0.0 3.8 %copy-start = (bf16[1,256,8,256]{3,2,1,0:T(8,128)(2,1)S(1)}, bf16[1,256,8,256]{3,2,1,0:T(8,128)(2,1)}, u32[]{:S(2)}) copy-start(bf16[1,256,8,256]{3,2,1,0:T(8,128)(2,1)} %param.5) | copy-start | bytes 3145732
  0.0 3.9 %copy-start.1 = (s32[1,2048,256]{2,1,0:T(8,128)S(1)}, s32[1,2048,256]{2,1,0:T(8,128)}, u32[]{:S(2)}) copy-start(s32[1,2048,256]{2,1,0:T(8,128)} %param.9) | copy-start | bytes 6291460
  2.0 2.1 %copy-start.3 = (bf16[1,64,64]{2,1,0:T(8,128)(2,1)S(1)}, bf16[1,64,64]{2,1,0:T(8,128)(2,1)}, u32[]{:S(2)}) copy-start(bf16[1,64,64]{2,1,0:T(8,128)(2,1)} %param.7) | copy-start | bytes 24580
  2.0 5.6 %collective-permute-start.1 = (bf16[2112,256]{1,0:T(8,128)(2,1)S(1)}, bf16[2112,256]{1,0:T(8,128)(2,1)S(1)}, u32[]{:S(2)}, u32[]{:S(2)}) collective-permute-start(bf16[2112,256]{1,0:T(8,128)(2,1)S(1)} %fusion.2.own_packed), channel_id=1, source_target_pairs={{0,1},{2,3},{4,5},{6,7},{8,9},{10,11},{12,13},{14,15},{16,17},{18,... | collective-permute-start | bytes 3244040 | tf_op jit(solution)/shard_map/ppermute | solution.py:236
  3.9 3.7 %collective-permute-start = (bf16[2048,256]{1,0:T(8,128)(2,1)S(1)}, bf16[2048,256]{1,0:T(8,128)(2,1)S(1)}, u32[]{:S(2)}, u32[]{:S(2)}) collective-permute-start(bf16[2048,256]{1,0:T(8,128)(2,1)S(1)} %bitcast.8), channel_id=1, source_target_pairs={{0,1},{1,0},{2,3},{3,2},{4,5},{5,4},{6,7},{7,6},{8,9},{9,8},{10,11... | collective-permute-start | bytes 3145736 | tf_op jit(solution)/shard_map/ppermute | solution.py:239
  4.2 40.9 %collective-permute-start.3 = (bf16[2112,256]{1,0:T(8,128)(2,1)S(1)}, bf16[2112,256]{1,0:T(8,128)(2,1)S(1)}, u32[]{:S(2)}, u32[]{:S(2)}) collective-permute-start(bf16[2112,256]{1,0:T(8,128)(2,1)S(1)} %fusion.3.own_packed), channel_id=1, source_target_pairs={{1,2},{3,4},{5,6},{7,8},{9,10},{11,12},{13,14},{15,16},{17,18},{19... | collective-permute-start | bytes 3244040 | tf_op jit(solution)/shard_map/ppermute | solution.py:236
  39.0 29.2 %collective-permute-start.2 = (bf16[2048,256]{1,0:T(8,128)(2,1)S(1)}, bf16[2048,256]{1,0:T(8,128)(2,1)S(1)}, u32[]{:S(2)}, u32[]{:S(2)}) collective-permute-start(bf16[2048,256]{1,0:T(8,128)(2,1)S(1)} %shard_map.55.own), channel_id=1, source_target_pairs={{1,2},{2,1},{3,4},{4,3},{5,6},{6,5},{7,8},{8,7},{9,10},{10,9},{11,... | collective-permute-start | bytes 3145736 | tf_op jit(solution)/shard_map/ppermute | solution.py:239

commit v3 on v2

--- a/solution.py
+++ b/solution.py
@@ -7,7 +7,7 @@
 from jax.experimental.pallas import tpu as pltpu
 from jax.sharding import PartitionSpec as P
 
-PANEL = 32
+PANEL = 64
 TILE = 8
 F32 = jnp.float32
 BF16 = jnp.bfloat16
@@ -100,8 +100,9 @@
             upper = jnp.where(lane_of >= start + PANEL, panel, 0.0)
             inside = (lane_of >= start) & (lane_of < start + PANEL)
             reached = jnp.where(inside & (lane_of > start + row_of), 0.0, panel)
-            update = dot(upper, reached, ((0,), (0,)), lax.Precision.HIGHEST)
-            work = jnp.where(inside, 0.0, work[PANEL:]) - update[start + PANEL :]
+            skip = (start + PANEL) // 128 * 128
+            update = dot(upper[:, skip:], reached, ((0,), (0,)), lax.Precision.HIGHEST)
+            work = jnp.where(inside, 0.0, work[PANEL:]) - update[start + PANEL - skip :]
     lower = jnp.concatenate(done, axis=0)
     keep = lax.broadcasted_iota(jnp.int32, (size, size), 0) >= lax.broadcasted_iota(jnp.int32, (size, size), 1)
     return jnp.where(keep, lower, 0.0)

time: 104 us -> 101 us (0.971)
  Pallas kernels: 66.7 us -> 63.9 us
    pallas_call x2, Pallas kernels: 66.7 us -> 63.9 us  [apply_layer(): pl.pallas_call(functools.partial(layer_kernel, parity, levels, bond), out...]
where the time goes in v3:
time: 101 us
  Pallas kernels  63.9 us (63%)
  waiting for transfers between devices  25.1 us (25%)
  starting transfers between devices  9.32 us (9%)
  other arithmetic  2.23 us (2%)
    pallas_call x2, Pallas kernels, apply_layer(): pl.pallas_call(functools.partial(layer_kernel, parity, levels, bond), out...  63.9 us
    ppermute x2, waiting for transfers between devices, per_device(): other = lax.ppermute(tensor, 'site', swaps)  25.1 us
    ppermute x2, starting transfers between devices, per_device(): other = lax.ppermute(tensor, 'site', swaps)  6.22 us
    ppermute x2, starting transfers between devices, per_device(): sent.append(lax.ppermute(packed, 'site', to_right))  3.1 us
    convert_element_type x2, other arithmetic, per_device(): packs.append(jnp.concatenate([sketch.astype(BF16), padded], axis=0))  2.08 us
  transfers between devices with their start and end apart: 4, of which 2 were waited for; matrix products, arithmetic and copies ran while one was open for 0% of the time, Pallas kernels for 30%

profile of v3, /device:TPU:4, one launch (start us, length us, event | category | flops | bytes accessed | tf_op | source)
XLA Modules:
  0.0 100.9 jit_solution(11406646124012688936)
XLA Ops:
  0.0 0.0 copy-start.2
  0.0 0.0 copy-start
  0.0 0.0 copy-start.1
  0.0 1.9 %convert_bitcast_fusion.1 = bf16[2048,256]{1,0:T(8,128)(2,1)S(1)} fusion(s32[1,2048,256]{2,1,0:T(8,128)} %param.8), kind=kLoop, calls=%fused_computation.6 | loop fusion | flops 524288 | bytes 3145728 | tf_op jit(solution)/shard_map/convert_element_type | solution.py:233
  1.9 0.0 copy-done.2
  1.9 0.1 fusion.2.own_packed
  2.0 0.0 copy-start.3
  2.0 1.8 %collective-permute-start.1 = (bf16[2112,256]{1,0:T(8,128)(2,1)S(1)}, bf16[2112,256]{1,0:T(8,128)(2,1)S(1)}, u32[]{:S(2)}, u32[]{:S(2)}) collective-permute-start(bf16[2112,256]{1,0:T(8,128)(2,1)S(1)} %fusion.2.own_packed), channel_id=1, source_target_pairs={{0,1},{2,3},{4,5},{6,7},{8,9},{10,11},{12,13},{14,15},{16,17},{18,... | collective-permute-start | bytes 3244040 | tf_op jit(solution)/shard_map/ppermute | solution.py:237
  3.8 0.0 copy-done
  3.9 0.1 collective-permute-start
  3.9 0.0 copy-done.1
  3.9 0.2 convert_bitcast_fusion
  4.1 0.0 copy-done.3
  4.1 0.1 fusion.3.own_packed
  4.2 1.3 %collective-permute-start.3 = (bf16[2112,256]{1,0:T(8,128)(2,1)S(1)}, bf16[2112,256]{1,0:T(8,128)(2,1)S(1)}, u32[]{:S(2)}, u32[]{:S(2)}) collective-permute-start(bf16[2112,256]{1,0:T(8,128)(2,1)S(1)} %fusion.3.own_packed), channel_id=1, source_target_pairs={{1,2},{3,4},{5,6},{7,8},{9,10},{11,12},{13,14},{15,16},{17,18},{19... | collective-permute-start | bytes 3244040 | tf_op jit(solution)/shard_map/ppermute | solution.py:237
  5.5 2.1 %collective-permute-done.other = bf16[2048,256]{1,0:T(8,128)(2,1)S(1)} collective-permute-done((bf16[2048,256]{1,0:T(8,128)(2,1)S(1)}, bf16[2048,256]{1,0:T(8,128)(2,1)S(1)}, u32[]{:S(2)}, u32[]{:S(2)}) %collective-permute-start) | collective-permute-done | bytes 1048608 | tf_op jit(solution)/shard_map/ppermute | solution.py:240
  7.6 0.0 collective-permute-done.1.other_packed
  7.6 30.0 %shard_map.55.own = bf16[2048,256]{1,0:T(8,128)(2,1)S(1)} custom-call(bf16[2048,256]{1,0:T(8,128)(2,1)S(1)} %bitcast.9, bf16[2048,256]{1,0:T(8,128)(2,1)S(1)} %collective-permute-done.other, bf16[2112,256]{1,0:T(8,128)(2,1)S(1)} %fusion.2.own_packed, bf16[2112,256]{1,0:T(8,128)(2,1)S(1)} %collective-permute-done.1.other_packed), custom_call_target="tpu_custom_call" | custom-call | flops 8589934592 | bytes 4194304 | tf_op jit(solution)/shard_map/pallas_call | solution.py:202
  37.6 6.2 %collective-permute-start.2 = (bf16[2048,256]{1,0:T(8,128)(2,1)S(1)}, bf16[2048,256]{1,0:T(8,128)(2,1)S(1)}, u32[]{:S(2)}, u32[]{:S(2)}) collective-permute-start(bf16[2048,256]{1,0:T(8,128)(2,1)S(1)} %shard_map.55.own), channel_id=1, source_target_pairs={{1,2},{2,1},{3,4},{4,3},{5,6},{6,5},{7,8},{8,7},{9,10},{10,9},{11,... | collective-permute-start | bytes 3145736 | tf_op jit(solution)/shard_map/ppermute | solution.py:240
  43.7 0.0 collective-permute-done.3.other_packed
  43.8 23.0 %collective-permute-done.2.other = bf16[2048,256]{1,0:T(8,128)(2,1)S(1)} collective-permute-done((bf16[2048,256]{1,0:T(8,128)(2,1)S(1)}, bf16[2048,256]{1,0:T(8,128)(2,1)S(1)}, u32[]{:S(2)}, u32[]{:S(2)}) %collective-permute-start.2) | collective-permute-done | bytes 1048608 | tf_op jit(solution)/shard_map/ppermute | solution.py:240
  66.8 33.9 %shard_map.56 = bf16[2048,256]{1,0:T(8,128)(2,1)} custom-call(bf16[2048,256]{1,0:T(8,128)(2,1)S(1)} %shard_map.55.own, bf16[2048,256]{1,0:T(8,128)(2,1)S(1)} %collective-permute-done.2.other, bf16[2112,256]{1,0:T(8,128)(2,1)S(1)} %fusion.3.own_packed, bf16[2112,256]{1,0:T(8,128)(2,1)S(1)} %collective-permute-done.3.other_packed), custom_call_target="tpu_custom_call" | custom-call | flops 8589934592 | bytes 4194304 | tf_op jit(solution)/shard_map/pallas_call | solution.py:202
Async XLA Ops:
  0.0 1.9 %copy-start.2 = (bf16[1,64,64]{2,1,0:T(8,128)(2,1)S(1)}, bf16[1,64,64]{2,1,0:T(8,128)(2,1)}, u32[]{:S(2)}) copy-start(bf16[1,64,64]{2,1,0:T(8,128)(2,1)} %param.6) | copy-start | bytes 24580
  0.0 3.8 %copy-start = (bf16[1,256,8,256]{3,2,1,0:T(8,128)(2,1)S(1)}, bf16[1,256,8,256]{3,2,1,0:T(8,128)(2,1)}, u32[]{:S(2)}) copy-start(bf16[1,256,8,256]{3,2,1,0:T(8,128)(2,1)} %param.5) | copy-start | bytes 3145732
  0.0 3.9 %copy-start.1 = (s32[1,2048,256]{2,1,0:T(8,128)S(1)}, s32[1,2048,256]{2,1,0:T(8,128)}, u32[]{:S(2)}) copy-start(s32[1,2048,256]{2,1,0:T(8,128)} %param.9) | copy-start | bytes 6291460
  2.0 2.1 %copy-start.3 = (bf16[1,64,64]{2,1,0:T(8,128)(2,1)S(1)}, bf16[1,64,64]{2,1,0:T(8,128)(2,1)}, u32[]{:S(2)}) copy-start(bf16[1,64,64]{2,1,0:T(8,128)(2,1)} %param.7) | copy-start | bytes 24580
  2.0 5.6 %collective-permute-start.1 = (bf16[2112,256]{1,0:T(8,128)(2,1)S(1)}, bf16[2112,256]{1,0:T(8,128)(2,1)S(1)}, u32[]{:S(2)}, u32[]{:S(2)}) collective-permute-start(bf16[2112,256]{1,0:T(8,128)(2,1)S(1)} %fusion.2.own_packed), channel_id=1, source_target_pairs={{0,1},{2,3},{4,5},{6,7},{8,9},{10,11},{12,13},{14,15},{16,17},{18,... | collective-permute-start | bytes 3244040 | tf_op jit(solution)/shard_map/ppermute | solution.py:237
  3.9 3.7 %collective-permute-start = (bf16[2048,256]{1,0:T(8,128)(2,1)S(1)}, bf16[2048,256]{1,0:T(8,128)(2,1)S(1)}, u32[]{:S(2)}, u32[]{:S(2)}) collective-permute-start(bf16[2048,256]{1,0:T(8,128)(2,1)S(1)} %bitcast.8), channel_id=1, source_target_pairs={{0,1},{1,0},{2,3},{3,2},{4,5},{5,4},{6,7},{7,6},{8,9},{9,8},{10,11... | collective-permute-start | bytes 3145736 | tf_op jit(solution)/shard_map/ppermute | solution.py:240
  4.2 39.5 %collective-permute-start.3 = (bf16[2112,256]{1,0:T(8,128)(2,1)S(1)}, bf16[2112,256]{1,0:T(8,128)(2,1)S(1)}, u32[]{:S(2)}, u32[]{:S(2)}) collective-permute-start(bf16[2112,256]{1,0:T(8,128)(2,1)S(1)} %fusion.3.own_packed), channel_id=1, source_target_pairs={{1,2},{3,4},{5,6},{7,8},{9,10},{11,12},{13,14},{15,16},{17,18},{19... | collective-permute-start | bytes 3244040 | tf_op jit(solution)/shard_map/ppermute | solution.py:237
  37.6 29.2 %collective-permute-start.2 = (bf16[2048,256]{1,0:T(8,128)(2,1)S(1)}, bf16[2048,256]{1,0:T(8,128)(2,1)S(1)}, u32[]{:S(2)}, u32[]{:S(2)}) collective-permute-start(bf16[2048,256]{1,0:T(8,128)(2,1)S(1)} %shard_map.55.own), channel_id=1, source_target_pairs={{1,2},{2,1},{3,4},{4,3},{5,6},{6,5},{7,8},{8,7},{9,10},{10,9},{11,... | collective-permute-start | bytes 3145736 | tf_op jit(solution)/shard_map/ppermute | solution.py:240
